TPU v7x, 32 devices: a whole 2x2x4 slice. The times are simulated.
32 devices in a mesh: fsdp: 8 (over z, y), rep: 4 (over x, core).
Axes of the slice: x: 2, y: 2, z: 4, core: 2. Of those that a mesh axis runs over, the one named last changes fastest.
Arguments:
- tokens: bfloat16 [8192, 1088], P(('fsdp', 'rep')), may hold values from -6 to 6
- lengths: int32 [32, 4], P(('fsdp', 'rep')), may hold values from 0 to 256, as said below
- attn_weights: bfloat16 [4352, 1088], P(('fsdp', 'rep'))
- vectors: bfloat16 [13056], P(('fsdp', 'rep'))
- up_weights: bfloat16 [4352, 1088], P(('fsdp', 'rep')), may hold values from -0.1875 to 0.1875
- down_weights: bfloat16 [4352, 1088], P(('fsdp', 'rep')), may hold values from -0.09375 to 0.09375
- cotangent: bfloat16 [8192, 1088], P(('fsdp', 'rep')), may hold values from -6 to 6
Outputs:
- out: bfloat16 [8192, 1088], P(('fsdp', 'rep'))
- grad_tokens: bfloat16 [8192, 1088], P(('fsdp', 'rep'))
- grad_attn_weights: float32 [4352, 1088], P(('fsdp', 'rep'))
- grad_vectors: float32 [13056], P(('fsdp', 'rep'))
- grad_up_weights: float32 [4352, 1088], P(('fsdp', 'rep'))
- grad_down_weights: float32 [4352, 1088], P(('fsdp', 'rep'))
Inputs may be any that keep to these rules, and one draw needn't show every extreme that they name: `lengths`: row p gives, in order from slot 0, the sequences packed into the blocks of pack p, which is held by device p of fsdp+rep (fsdp major); a row sums to at most 256 and the slots after its sum are empty; in every draw one row, drawn from the seed, is a single sequence of 256 tokens followed by zeros.
All inputs are finite; a program needn't handle non-finite values.
Results may differ from a plain program's by a relative error of at most 0.013.
Values may be sent and summed in bfloat16 or wider, within the bound.
A program may use at most 192 MiB of HBM per device.

v0:
```python
import jax
import jax.numpy as jnp
from jax import lax
from jax.sharding import PartitionSpec as P

HEADS = 17
HEAD_DIM = 64
FF = 4352


epsilon = 1e-05
negative = -1e30


def for_sending(shard):
    return jax.tree.map(lambda a: a.astype(jnp.bfloat16) if a.dtype == jnp.float32 else a, shard)


def contract(left, right, left_dim, right_dim):
    return lax.dot_general(
        left, right, (((left_dim,), (right_dim,)), ((), ())), preferred_element_type=jnp.float32
    )


def normalize(values):
    center = values - jnp.mean(values, axis=1, keepdims=True)
    scaled = lax.rsqrt(jnp.mean(center * center, axis=1, keepdims=True) + epsilon)
    return (center * scaled, scaled)


def norm_back(grad_normed, normed, scaled, gain):
    scaled_grad = grad_normed * gain
    return scaled * (
        scaled_grad
        - jnp.mean(scaled_grad, axis=1, keepdims=True)
        - normed * jnp.mean(scaled_grad * normed, axis=1, keepdims=True)
    )


def visible(segment, span_rows):
    row_ids = lax.iota(jnp.int32, span_rows)[:, None]
    col_ids = lax.iota(jnp.int32, segment.shape[0])[None, :]
    same_seg = segment[:, None] == segment[None, :]
    return same_seg & (col_ids <= row_ids)


def split_heads(matrix):
    return matrix.reshape(matrix.shape[0], HEADS, HEAD_DIM).transpose(1, 0, 2)


def join_heads(stacked):
    return stacked.transpose(1, 0, 2).reshape(stacked.shape[1], HEADS * HEAD_DIM)


def by_owner(matrix, outer_count, inner_count):
    slot_count, width = matrix.shape
    block_width = width // (outer_count * inner_count)
    return matrix.reshape(slot_count, outer_count, inner_count, block_width).transpose(0, 2, 1, 3)


def head_forward(head_parts, segment, span_rows):
    queries, key_heads, value_heads = head_parts
    factor = HEAD_DIM ** (-0.5)
    allowed = visible(segment, span_rows)
    raw_scores = contract(queries, key_heads, 1, 1)
    scores = jnp.where(allowed, raw_scores * factor, negative)
    row_peak = jnp.max(scores, axis=1, keepdims=True)
    exp_scores = jnp.exp(scores - row_peak)
    row_total = jnp.sum(exp_scores, axis=1, keepdims=True)
    prob_low = (exp_scores / row_total).astype(jnp.bfloat16)
    outputs = [contract(prob_low, value_heads, 1, 0)]
    totals = [row_peak + jnp.log(row_total)]
    return (jnp.concatenate(outputs, axis=0).astype(jnp.bfloat16), jnp.concatenate(totals, axis=0))


def head_backward(head_parts, segment, span_rows):
    queries, key_heads, value_heads, totals, grad_mixed = head_parts
    factor = HEAD_DIM ** (-0.5)
    grad_keys = jnp.zeros(key_heads.shape, jnp.float32)
    grad_values = jnp.zeros(value_heads.shape, jnp.float32)
    allowed = visible(segment, span_rows)
    grad_rows = grad_mixed[0:span_rows]
    raw_scores = contract(queries, key_heads, 1, 1)
    probs = jnp.where(allowed, jnp.exp(raw_scores * factor - totals[0:span_rows]), 0.0)
    grad_probs = contract(grad_rows, value_heads, 1, 1)
    row_delta = jnp.sum(probs * grad_probs, axis=1, keepdims=True)
    grad_scores = (probs * (grad_probs - row_delta) * factor).astype(jnp.bfloat16)
    grad_queries = [contract(grad_scores, key_heads, 1, 0)]
    grad_keys = grad_keys + contract(grad_scores, queries, 0, 0)
    grad_values = grad_values + contract(probs.astype(jnp.bfloat16), grad_rows, 0, 0)
    return (jnp.concatenate(grad_queries, axis=0), grad_keys, grad_values)


def local(tokens, lengths, attn_weights, vectors, up_weights, down_weights, cotangent):
    attn_full, vector_full = (
        lax.all_gather(attn_weights, ("fsdp", "rep"), axis=0, tiled=True),
        lax.all_gather(vectors, ("fsdp", "rep"), axis=0, tiled=True),
    )
    params = vector_full.astype(jnp.float32)
    slot_count, model_width = tokens.shape
    span_rows = min(512, slot_count)
    gain_one = params[0:model_width]
    shift_one = params[model_width : 2 * model_width]
    query_bias = params[2 * model_width : 3 * model_width]
    value_bias = params[3 * model_width : 4 * model_width]
    out_bias = params[4 * model_width : 5 * model_width]
    gain_two = params[5 * model_width : 6 * model_width]
    shift_two = params[6 * model_width : 7 * model_width]
    up_bias = params[7 * model_width : 7 * model_width + FF]
    down_bias = params[7 * model_width + FF :]
    seq_ends = jnp.cumsum(lengths[0])
    positions = lax.iota(jnp.int32, slot_count)
    segment = jnp.sum((positions[:, None] >= seq_ends[None, :]).astype(jnp.int32), axis=1)
    live_rows = (positions < seq_ends[-1]).astype(jnp.float32)[:, None]
    inputs = tokens.astype(jnp.float32)
    normed_one, scaled_one = normalize(inputs)
    hidden_one = (normed_one * gain_one + shift_one).astype(jnp.bfloat16)
    qkv_bias = jnp.concatenate([query_bias, jnp.zeros_like(query_bias), value_bias])
    projected = (contract(hidden_one, attn_full[: 3 * model_width], 1, 1) + qkv_bias).astype(
        jnp.bfloat16
    )
    queries = split_heads(projected[:, :model_width])
    key_heads = split_heads(projected[:, model_width : 2 * model_width])
    value_heads = split_heads(projected[:, 2 * model_width :])

    def attend_forward(head_parts):
        return head_forward(head_parts, segment, span_rows)

    mixed_heads, totals = lax.map(attend_forward, (queries, key_heads, value_heads))
    mixed = join_heads(mixed_heads)
    attended = contract(mixed, attn_full[3 * model_width :], 1, 1) + out_bias
    residual = inputs + attended
    normed_two, scaled_two = normalize(residual)
    hidden_two = (normed_two * gain_two + shift_two).astype(jnp.bfloat16)
    up_full, down_full = (
        lax.all_gather(up_weights, ("fsdp", "rep"), axis=0, tiled=True),
        lax.all_gather(down_weights, ("fsdp", "rep"), axis=0, tiled=True),
    )
    upward = contract(hidden_two, up_full, 1, 1) + up_bias
    activated = jax.nn.gelu(upward, approximate=False).astype(jnp.bfloat16)
    output = (residual + contract(activated, down_full, 1, 0) + down_bias) * live_rows
    up_back, down_back = (
        lax.all_gather(up_weights, ("fsdp", "rep"), axis=0, tiled=True),
        lax.all_gather(down_weights, ("fsdp", "rep"), axis=0, tiled=True),
    )
    grad_output = cotangent.astype(jnp.float32) * live_rows
    grad_down_in = grad_output.astype(jnp.bfloat16)
    grad_down_bias = jnp.sum(grad_down_in.astype(jnp.float32), axis=0)
    grad_act = contract(grad_down_in, down_back, 1, 1)

    def gelu_exact(values):
        return jax.nn.gelu(values, approximate=False)

    grad_upward = jax.vjp(gelu_exact, upward)[1](grad_act)[0]
    grad_up_in = grad_upward.astype(jnp.bfloat16)
    grad_up_bias = jnp.sum(grad_up_in.astype(jnp.float32), axis=0)
    grad_hidden_two = contract(grad_up_in, up_back, 1, 0)
    grad_gain_two = jnp.sum(grad_hidden_two * normed_two, axis=0)
    grad_shift_two = jnp.sum(grad_hidden_two, axis=0)
    grad_residual = grad_output + norm_back(grad_hidden_two, normed_two, scaled_two, gain_two)
    grad_attended = grad_residual.astype(jnp.bfloat16)
    attn_back = lax.all_gather(attn_weights, ("fsdp", "rep"), axis=0, tiled=True)
    grad_out_bias = jnp.sum(grad_attended.astype(jnp.float32), axis=0)
    grad_mixed = contract(grad_attended, attn_back[3 * model_width :], 1, 0).astype(jnp.bfloat16)

    def attend_backward(head_parts):
        return head_backward(head_parts, segment, span_rows)

    grad_q_heads, grad_k_heads, grad_v_heads = lax.map(
        attend_backward, (queries, key_heads, value_heads, totals, split_heads(grad_mixed))
    )
    grad_projected = jnp.concatenate(
        [join_heads(grad_q_heads), join_heads(grad_k_heads), join_heads(grad_v_heads)], axis=1
    ).astype(jnp.bfloat16)
    bias_sums = jnp.sum(grad_projected.astype(jnp.float32), axis=0)
    grad_hidden_one = contract(grad_projected, attn_back[: 3 * model_width], 1, 0)
    grad_gain_one = jnp.sum(grad_hidden_one * normed_one, axis=0)
    grad_shift_one = jnp.sum(grad_hidden_one, axis=0)
    grad_inputs = grad_residual + norm_back(grad_hidden_one, normed_one, scaled_one, gain_one)
    outer_count = lax.axis_size("fsdp")
    inner_count = lax.axis_size("rep")
    inner_index = lax.axis_index("rep")
    attn_left = jnp.concatenate([grad_projected, grad_attended], axis=1)
    attn_block = attn_left.shape[1] // (outer_count * inner_count)
    unit_block = grad_up_in.shape[1] // (outer_count * inner_count)
    bundle = jnp.concatenate(
        [
            by_owner(attn_left, outer_count, inner_count),
            by_owner(grad_up_in, outer_count, inner_count),
            by_owner(activated, outer_count, inner_count),
        ],
        axis=3,
    )
    bundle_width = bundle.shape[3]
    bundle = bundle.reshape(slot_count, inner_count * outer_count * bundle_width)
    received = lax.all_to_all(bundle, "rep", split_axis=1, concat_axis=0, tiled=True)
    received = received.reshape(received.shape[0], outer_count, bundle_width)
    attn_cols = received[:, :, :attn_block].reshape(received.shape[0], outer_count * attn_block)
    up_cols = received[:, :, attn_block : attn_block + unit_block].reshape(
        received.shape[0], outer_count * unit_block
    )
    act_cols = received[:, :, attn_block + unit_block :].reshape(
        received.shape[0], outer_count * unit_block
    )
    outer_ids = lax.iota(jnp.int32, outer_count)[:, None]
    inner_ids = lax.iota(jnp.int32, attn_block)[None, :]
    feature_ids = ((outer_ids * inner_count + inner_index) * attn_block + inner_ids).reshape(
        outer_count * attn_block
    )
    is_projection = (feature_ids < 3 * model_width)[None, :]
    start_sums = (
        jnp.zeros((outer_count * attn_block, model_width), jnp.float32),
        jnp.zeros((outer_count * unit_block, model_width), jnp.float32),
        jnp.zeros((outer_count * unit_block, model_width), jnp.float32),
    )
    piece_h1 = lax.all_gather(hidden_one, "rep", axis=0, tiled=True)
    piece_mixed = lax.all_gather(for_sending(mixed), "rep", axis=0, tiled=True)
    piece_h2 = lax.all_gather(hidden_two, "rep", axis=0, tiled=True)
    piece_dd = lax.all_gather(grad_down_in, "rep", axis=0, tiled=True)
    zero_low = jnp.zeros_like(attn_cols)
    left_proj = jnp.where(is_projection, attn_cols, zero_low)
    left_out = jnp.where(is_projection, zero_low, attn_cols)
    attn_total = (
        start_sums[0] + contract(left_proj, piece_h1, 0, 0) + contract(left_out, piece_mixed, 0, 0)
    )
    up_total = start_sums[1] + contract(up_cols, piece_h2, 0, 0)
    down_total = start_sums[2] + contract(act_cols, piece_dd, 0, 0)
    attn_shard, up_shard, down_shard = (
        lax.psum_scatter(attn_total, "fsdp", scatter_dimension=0, tiled=True),
        lax.psum_scatter(up_total, "fsdp", scatter_dimension=0, tiled=True),
        lax.psum_scatter(down_total, "fsdp", scatter_dimension=0, tiled=True),
    )
    grad_params = jnp.concatenate(
        [
            grad_gain_one,
            grad_shift_one,
            bias_sums[:model_width],
            bias_sums[2 * model_width :],
            grad_out_bias,
            grad_gain_two,
            grad_shift_two,
            grad_up_bias,
            grad_down_bias,
        ]
    )
    vector_shard = lax.psum_scatter(grad_params, ("fsdp", "rep"), scatter_dimension=0, tiled=True)
    return (
        output.astype(jnp.bfloat16),
        grad_inputs.astype(jnp.bfloat16),
        attn_shard,
        vector_shard,
        up_shard,
        down_shard,
    )


def solution(mesh):
    return jax.shard_map(
        local,
        mesh=mesh,
        in_specs=(
            P(("fsdp", "rep"), None),
            P(("fsdp", "rep"), None),
            P(("fsdp", "rep"), None),
            P(("fsdp", "rep")),
            P(("fsdp", "rep"), None),
            P(("fsdp", "rep"), None),
            P(("fsdp", "rep"), None),
        ),
        out_specs=(
            P(("fsdp", "rep"), None),
            P(("fsdp", "rep"), None),
            P(("fsdp", "rep"), None),
            P(("fsdp", "rep")),
            P(("fsdp", "rep"), None),
            P(("fsdp", "rep"), None),
        ),
        check_vma=False,
    )
```

profile of v0, /device:TPU:0, one launch (start us, length us, event | category | flops | bytes accessed | tf_op | source)
XLA Modules:
  0.0 895.4 jit_solution(2756972596517927532)
XLA Ops:
  10.4 42.8 %all-reduce = bf16[13056]{0:T(1024)(128)(2,1)S(1)} all-reduce(bf16[13056]{0:T(1024)(128)(2,1)S(1)} %dynamic-update-slice), channel_id=1, replica_groups=mesh['fsdp'=8,'rep'=4] {'fsdp','rep'}, use_global_device_ids=true, to_apply=%add | all-reduce | flops 13056 | bytes 52224
  56.5 42.6 %all-gather.8.cloned.1.call-done = bf16[4352,1088]{1,0:T(8,128)(2,1)} async-done(((bf16[136,1088]{1,0:T(8,128)(2,1)}), bf16[4352,1088]{1,0:T(8,128)(2,1)}) %all-gather.8.cloned.1.call-update) | async-done | bytes 9469968 | tf_op jit(solution)/shard_map/all_gather | solution.py:96
  99.2 5.5 fusion.50
  108.4 37.9 %while.26 = (s32[]{:T(128)}, bf16[17,256,64]{1,2,0:T(8,128)(2,1)S(1)}, f32[17,256,1]{1,2,0:T(1,128)S(1)}, s32[256]{0:T(256)S(1)}, bf16[17,256,64]{2,1,0:T(8,128)...) while((s32[]{:T(128)}, bf16[17,256,64]{1,2,0:T(8,128)(2,1)S(1)}, ...), condition=%wide.region_7.8_spmd, body=%wide.region_4.7_spmd.sunk | while | flops 17514240 | bytes 1030233 | solution.py:129
  153.5 31.8 %all-gather.10.cloned.1.call-done = bf16[4352,1088]{1,0:T(8,128)(2,1)} async-done(((bf16[136,1088]{1,0:T(8,128)(2,1)}), bf16[4352,1088]{1,0:T(8,128)(2,1)}) %all-gather.10.cloned.1.call-update) | async-done | bytes 9469968 | tf_op jit(solution)/shard_map/all_gather | solution.py:136
  185.2 10.8 %convolution_add_fusion.1 = f32[256,4352]{1,0:T(8,128)} fusion(bf16[256,1088]{0,1:T(8,128)(2,1)S(1)} %copy-done.11, bf16[4352,1088]{1,0:T(8,128)(2,1)} %all-gather.10.cloned.1.call-done, f32[4352]{0:T(1024)S(1)} %slice.95), kind=kOutput, calls=%fused_computation.61 | convolution fusion | flops 2425421824 | bytes 14500864 | tf_op jit(solution)/shard_map/dot_general | solution.py:20
  196.1 75.4 %all-gather.12.cloned.1.call-done = bf16[4352,1088]{1,0:T(8,128)(2,1)} async-done(((bf16[136,1088]{1,0:T(8,128)(2,1)}), bf16[4352,1088]{1,0:T(8,128)(2,1)}) %all-gather.12.cloned.1.call-update) | async-done | bytes 9469968 | tf_op jit(solution)/shard_map/all_gather | solution.py:137
  271.5 17.3 %convert_reduce_fusion = (f32[4352]{0:T(1024)S(1)}, bf16[256,4352]{1,0:T(8,128)(2,1)S(1)}, f32[256,4352]{1,0:T(8,128)}) fusion(f32[256,4352]{1,0:T(8,128)} %convolution_add_fusion.1, bf16[256,1088]{0,1:T(8,128)(2,1)S(1)} %get-tuple-element.146, bf16[4352,1088]{1,0:T(8,128)(2,1)} %all-gather.12.cloned.1.call-done), kind=kOutput, calls=%fused_computation.69 | convolution fusion | flops 2506747648 | bytes 21185536 | tf_op jit(solution)/shard_map/dot_general | solution.py:20
  288.8 9.0 %multiply_reduce_fusion.1 = (f32[1088]{0:T(1024)S(1)}, f32[256]{0:T(256)S(1)}, f32[256]{0:T(256)S(1)}, f32[1088]{0:T(1024)S(1)}, f32[256,1088]{0,1:T(8,128)S(1)}) fusion(f32[256,1088]{0,1:T(8,128)S(1)} %get-tuple-element.175, f32[256]{0:T(256)S(1)} %add_rsqrt_fusion, f32[256]{0:T(256)S(1)} %broadcast_multiply_fusion.4, f32[1088]{0:T(1024)S(1)} %get-tuple-element.165, ...), kind=kOutput, calls=%fused_computation.117 | convolution fusion | flops 2426811904 | bytes 13943552 | tf_op jit(solution)/shard_map/dot_general | solution.py:20
  302.3 107.8 %while.27 = (s32[]{:T(128)}, bf16[17,256,64]{1,2,0:T(8,128)(2,1)}, bf16[17,256,64]{1,2,0:T(8,128)(2,1)}, bf16[17,256,64]{1,2,0:T(8,128)(2,1)}, s32[256]{0:T(256)...) while((s32[]{:T(128)}, bf16[17,256,64]{1,2,0:T(8,128)(2,1)}, ...), condition=%wide.region_14.15_spmd, body=%wide.region_12.14_spmd.sunk | while | flops 42794752 | bytes 2633841 | solution.py:169
  438.4 88.6 %all-to-all-done = bf16[256,4,3264]{0,2,1:T(8,128)(2,1)} async-done(((bf16[256,4,3264]{0,2,1:T(8,128)(2,1)}), bf16[256,4,3264]{0,2,1:T(8,128)(2,1)}, u32[]{:S(2)}, u32[]{:S(2)}) %all-to-all-start) | async-done | bytes 6684704 | tf_op jit(solution)/shard_map/all_to_all | solution.py:196
  527.0 27.7 %copy.42 = bf16[4,256,3264]{1,0,2:T(4,128)(2,1)} copy(bf16[4,256,3264]{1,2,0:T(8,128)(2,1)} %bitcast.42) | data formatting | bytes 13369344 | tf_op jit(solution)/shard_map/all_to_all | solution.py:196
  554.7 12.7 %reshape.193 = bf16[1024,8,408]{0,2,1:T(8,128)(2,1)} reshape(bf16[4,256,3264]{1,0,2:T(4,128)(2,1)} %copy.42) | data formatting | bytes 13369344 | tf_op jit(solution)/shard_map/reshape | solution.py:197
  567.4 6.2 fusion.87
  573.6 7.6 fusion.93
  584.0 7.8 fusion.92
  591.8 7.3 convolution_add_fusion
  600.7 6.5 fusion.94
  609.2 8.1 fusion.78
  617.4 40.4 %all-reduce.2 = f32[13056]{0:T(1024)S(1)} all-reduce(f32[13056]{0:T(1024)S(1)} %concatenate.21), channel_id=3, replica_groups=mesh['fsdp'=8,'rep'=4] {'fsdp','rep'}, use_global_device_ids=true, to_apply=%region_26.27.clone | all-reduce | flops 13056 | bytes 104448
  661.4 8.7 fusion.62
  670.1 11.5 %reduce-scatter.12.cloned.1.call-done = f32[136,1088]{1,0:T(8,128)} async-done(((f32[1088,1088]{1,0:T(8,128)}), f32[136,1088]{1,0:T(8,128)}) %reduce-scatter.12.cloned.1.call-update) | async-done | bytes 591888
  681.6 103.8 %reduce-scatter.10.cloned.1.call-done = f32[136,1088]{1,0:T(8,128)} async-done(((f32[1088,1088]{1,0:T(8,128)}), f32[136,1088]{1,0:T(8,128)}) %reduce-scatter.10.cloned.1.call-update) | async-done | bytes 591888
  785.3 103.0 %reduce-scatter.14.cloned.1.call-done = f32[136,1088]{1,0:T(8,128)} async-done(((f32[1088,1088]{1,0:T(8,128)}), f32[136,1088]{1,0:T(8,128)}) %reduce-scatter.14.cloned.1.call-update) | async-done | bytes 591888
  (318 shorter events, 204.8 us)
Async XLA Ops:
  7.2 48.9 %copy-start.2 = (bf16[256,1088]{0,1:T(8,128)(2,1)S(1)}, bf16[256,1088]{0,1:T(8,128)(2,1)}, u32[]{:S(2)}) copy-start(bf16[256,1088]{0,1:T(8,128)(2,1)} %param.11) | copy-start | bytes 1671172
  7.2 48.6 %copy-start.18 = (s32[1,4]{1,0:T(1,128)S(1)}, s32[1,4]{1,0:T(1,128)}, u32[]{:S(2)}) copy-start(s32[1,4]{1,0:T(1,128)} %param.12) | copy-start | bytes 52
  7.2 92.0 %all-gather.8.cloned.1.call-start = ((), (), s32[]{:S(2)}) async-start(), calls=%async_computation.4 | async-start | bytes 10340352 | tf_op jit(solution)/shard_map/all_gather | solution.py:96
  7.9 177.3 %all-gather.10.cloned.1.call-start = ((), (), s32[]{:S(2)}) async-start(), calls=%async_computation.5 | async-start | bytes 10340352 | tf_op jit(solution)/shard_map/all_gather | solution.py:136
  8.7 262.8 %all-gather.12.cloned.1.call-start = ((), (), s32[]{:S(2)}) async-start(), calls=%async_computation.6 | async-start | bytes 10340352 | tf_op jit(solution)/shard_map/all_gather | solution.py:137
  9.4 564.2 %all-gather.18.cloned.1.call-start = ((), (), s32[]{:S(2)}) async-start(), calls=%async_computation.9 | async-start | bytes 2785280 | tf_op jit(solution)/shard_map/all_gather | solution.py:218
  56.4 48.2 %copy-start.13 = (bf16[256,1088]{0,1:T(8,128)(2,1)}, bf16[256,1088]{0,1:T(8,128)(2,1)S(1)}, u32[]{:S(2)}) copy-start(bf16[256,1088]{0,1:T(8,128)(2,1)S(1)} %fusion.72) | copy-start | bytes 1671172
  146.4 3.2 copy-start.15
  146.4 3.2 copy-start.17
  149.6 3.6 copy-start.4
  151.0 34.2 %copy-start.11 = (bf16[256,1088]{0,1:T(8,128)(2,1)S(1)}, bf16[256,1088]{0,1:T(8,128)(2,1)}, u32[]{:S(2)}) copy-start(bf16[256,1088]{0,1:T(8,128)(2,1)} %add_convert_fusion.1) | copy-start | bytes 1671172
  151.0 433.0 %all-gather.14.cloned.1.call-start = ((), (), s32[]{:S(2)}) async-start(), calls=%async_computation.7 | async-start | bytes 2785280 | tf_op jit(solution)/shard_map/all_gather | solution.py:216
  151.6 440.2 %all-gather.16.cloned.1.call-start = ((), (), s32[]{:S(2)}) async-start(), calls=%async_computation.8 | async-start | bytes 2785280 | tf_op jit(solution)/shard_map/all_gather | solution.py:217
  153.5 118.0 %copy-start.14 = (bf16[256,1088]{0,1:T(8,128)(2,1)}, bf16[256,1088]{0,1:T(8,128)(2,1)S(1)}, u32[]{:S(2)}) copy-start(bf16[256,1088]{0,1:T(8,128)(2,1)S(1)} %get-tuple-element.146) | copy-start | bytes 1671172
  288.8 9.0 %copy-start.12 = (bf16[256,4352]{1,0:T(8,128)(2,1)}, bf16[256,4352]{1,0:T(8,128)(2,1)S(1)}, u32[]{:S(2)}) copy-start(bf16[256,4352]{1,0:T(8,128)(2,1)S(1)} %get-tuple-element.148) | copy-start | bytes 6684676
  297.8 3.7 copy-start.6
  432.3 94.7 %all-to-all-start = ((bf16[256,4,3264]{0,2,1:T(8,128)(2,1)}), bf16[256,4,3264]{0,2,1:T(8,128)(2,1)}, u32[]{:S(2)}, u32[]{:S(2)}) async-start(bf16[256,4,3264]{0,2,1:T(8,128)(2,1)} %bitcast.152), calls=%async_computation | async-start | bytes 13369344 | tf_op jit(solution)/shard_map/all_to_all | solution.py:196
  437.6 161.5 %all-gather.20.cloned.1.call-start = ((), (), s32[]{:S(2)}) async-start(), calls=%async_computation.10 | async-start | bytes 2785280 | tf_op jit(solution)/shard_map/all_gather | solution.py:219
  438.4 243.2 %reduce-scatter.12.cloned.1.call-start = ((), (), s32[]{:S(2)}) async-start(), calls=%async_computation.12 | async-start | bytes 5640192
  581.2 204.1 %reduce-scatter.10.cloned.1.call-start = ((), (), s32[]{:S(2)}) async-start(), calls=%async_computation.11 | async-start | bytes 5640192
  584.0 7.8 copy-start.9
  599.1 289.3 %reduce-scatter.14.cloned.1.call-start = ((), (), s32[]{:S(2)}) async-start(), calls=%async_computation.13 | async-start | bytes 5640192
  609.2 49.2 %copy-start.5 = (bf16[256,1088]{0,1:T(8,128)(2,1)S(1)}, bf16[256,1088]{0,1:T(8,128)(2,1)}, u32[]{:S(2)}) copy-start(bf16[256,1088]{0,1:T(8,128)(2,1)} %param.17) | copy-start | bytes 1671172
  609.2 49.2 %copy-start.7 = (f32[256,1088]{0,1:T(8,128)S(1)}, f32[256,1088]{0,1:T(8,128)}, u32[]{:S(2)}) copy-start(f32[256,1088]{0,1:T(8,128)} %copy-done.6) | copy-start | bytes 3342340
  (6 other events, 14.9 us)
Sparse Core Ops, SparseCore 0:
  10.9 88.1 all-gather.7
  102.1 83.1 all-gather.9
  188.2 83.2 all-gather.11
  273.4 22.1 all-gather.17
  297.6 23.5 all-gather.13
  422.9 24.7 all-gather.15
  449.3 37.3 all-gather.19
  581.3 100.1 reduce-scatter.11
  686.2 99.0 reduce-scatter.9
  789.4 98.9 reduce-scatter.13
where the time goes:
time: 907 us; the launch traced here: 895 us
  waiting for transfers between devices  460 us (51%)
  matrix products  237 us (26%)
  blocking collectives  83.2 us (9%)
  local copies, waits for them, and re-layouts  66.5 us (7%)
  other arithmetic  27 us (3%)
  between operations  14.8 us (2%)
    dot_general x131, matrix products, contract(): lax.dot_general(left, right, (((left_dim,), (right_dim,)), ((), ())), pre...  237 us
    unnamed x13, waiting for transfers between devices  222 us
    all_to_all x1, waiting for transfers between devices, local(): lax.all_to_all(bundle, 'rep', split_axis=1, concat_axis=0, tiled=True)  88.6 us
    unnamed x2, blocking collectives  83.2 us
    all_gather x1, waiting for transfers between devices, local(): lax.all_gather(down_weights, ('fsdp', 'rep'), axis=0, tiled=True)  75.4 us
    all_gather x1, waiting for transfers between devices, local(): lax.all_gather(attn_weights, ('fsdp', 'rep'), axis=0, tiled=True)  42.6 us
    all_gather x1, waiting for transfers between devices, local(): lax.all_gather(up_weights, ('fsdp', 'rep'), axis=0, tiled=True)  31.8 us
    all_to_all x1, local copies, waits for them, and re-layouts, local(): lax.all_to_all(bundle, 'rep', split_axis=1, concat_axis=0, tiled=True)  27.7 us
  transfers between devices with their start and end apart: 11, of which 7 were waited for; matrix products, arithmetic and copies ran while one was open for 37% of the time, Pallas kernels for 0%

commit v1 on v0

--- a/solution.py
+++ b/solution.py
@@ -108,7 +108,9 @@
     shift_two = params[6 * model_width : 7 * model_width]
     up_bias = params[7 * model_width : 7 * model_width + FF]
     down_bias = params[7 * model_width + FF :]
-    seq_ends = jnp.cumsum(lengths[0])
+    seq_count = lengths.shape[1]
+    upto = lax.iota(jnp.int32, seq_count)[:, None] >= lax.iota(jnp.int32, seq_count)[None, :]
+    seq_ends = jnp.sum(jnp.where(upto, lengths, 0), axis=1)
     positions = lax.iota(jnp.int32, slot_count)
     segment = jnp.sum((positions[:, None] >= seq_ends[None, :]).astype(jnp.int32), axis=1)
     live_rows = (positions < seq_ends[-1]).astype(jnp.float32)[:, None]

time: 907 us -> 907 us (level)
  no operation moved by 1% of the time
where the time goes in v1:
time: 907 us; the launch traced here: 895 us
  waiting for transfers between devices  460 us (51%)
  matrix products  237 us (26%)
  blocking collectives  83.2 us (9%)
  local copies, waits for them, and re-layouts  66.5 us (7%)
  other arithmetic  26.9 us (3%)
  between operations  14.8 us (2%)
    dot_general x131, matrix products, contract(): lax.dot_general(left, right, (((left_dim,), (right_dim,)), ((), ())), pre...  237 us
    unnamed x13, waiting for transfers between devices  222 us
    all_to_all x1, waiting for transfers between devices, local(): lax.all_to_all(bundle, 'rep', split_axis=1, concat_axis=0, tiled=True)  88.6 us
    unnamed x2, blocking collectives  83.2 us
    all_gather x1, waiting for transfers between devices, local(): lax.all_gather(down_weights, ('fsdp', 'rep'), axis=0, tiled=True)  75.4 us
    all_gather x1, waiting for transfers between devices, local(): lax.all_gather(attn_weights, ('fsdp', 'rep'), axis=0, tiled=True)  42.7 us
    all_gather x1, waiting for transfers between devices, local(): lax.all_gather(up_weights, ('fsdp', 'rep'), axis=0, tiled=True)  31.8 us
    all_to_all x1, local copies, waits for them, and re-layouts, local(): lax.all_to_all(bundle, 'rep', split_axis=1, concat_axis=0, tiled=True)  27.7 us
  transfers between devices with their start and end apart: 11, of which 7 were waited for; matrix products, arithmetic and copies ran while one was open for 37% of the time, Pallas kernels for 0%

profile of v1, /device:TPU:0, one launch (start us, length us, event | category | flops | bytes accessed | tf_op | source)
XLA Modules:
  0.0 895.4 jit_solution(4535174679910639292)
XLA Ops:
  10.4 42.8 %all-reduce = bf16[13056]{0:T(1024)(128)(2,1)S(1)} all-reduce(bf16[13056]{0:T(1024)(128)(2,1)S(1)} %dynamic-update-slice), channel_id=1, replica_groups=mesh['fsdp'=8,'rep'=4] {'fsdp','rep'}, use_global_device_ids=true, to_apply=%add | all-reduce | flops 13056 | bytes 52224
  56.5 42.7 %all-gather.8.cloned.1.call-done = bf16[4352,1088]{1,0:T(8,128)(2,1)} async-done(((bf16[136,1088]{1,0:T(8,128)(2,1)}), bf16[4352,1088]{1,0:T(8,128)(2,1)}) %all-gather.8.cloned.1.call-update) | async-done | bytes 9469968 | tf_op jit(solution)/shard_map/all_gather | solution.py:96
  99.2 5.5 fusion.50
  108.4 37.9 %while.26 = (s32[]{:T(128)}, bf16[17,256,64]{1,2,0:T(8,128)(2,1)S(1)}, f32[17,256,1]{1,2,0:T(1,128)S(1)}, s32[256]{0:T(256)S(1)}, bf16[17,256,64]{2,1,0:T(8,128)...) while((s32[]{:T(128)}, bf16[17,256,64]{1,2,0:T(8,128)(2,1)S(1)}, ...), condition=%wide.region_7.8_spmd, body=%wide.region_4.7_spmd.sunk | while | flops 17514240 | bytes 1030233 | solution.py:131
  153.5 31.8 %all-gather.10.cloned.1.call-done = bf16[4352,1088]{1,0:T(8,128)(2,1)} async-done(((bf16[136,1088]{1,0:T(8,128)(2,1)}), bf16[4352,1088]{1,0:T(8,128)(2,1)}) %all-gather.10.cloned.1.call-update) | async-done | bytes 9469968 | tf_op jit(solution)/shard_map/all_gather | solution.py:138
  185.2 10.8 %convolution_add_fusion.1 = f32[256,4352]{1,0:T(8,128)} fusion(bf16[256,1088]{0,1:T(8,128)(2,1)S(1)} %copy-done.11, bf16[4352,1088]{1,0:T(8,128)(2,1)} %all-gather.10.cloned.1.call-done, f32[4352]{0:T(1024)S(1)} %slice.94), kind=kOutput, calls=%fused_computation.61 | convolution fusion | flops 2425421824 | bytes 14500864 | tf_op jit(solution)/shard_map/dot_general | solution.py:20
  196.1 75.4 %all-gather.12.cloned.1.call-done = bf16[4352,1088]{1,0:T(8,128)(2,1)} async-done(((bf16[136,1088]{1,0:T(8,128)(2,1)}), bf16[4352,1088]{1,0:T(8,128)(2,1)}) %all-gather.12.cloned.1.call-update) | async-done | bytes 9469968 | tf_op jit(solution)/shard_map/all_gather | solution.py:139
  271.5 17.3 %convert_reduce_fusion = (f32[4352]{0:T(1024)S(1)}, bf16[256,4352]{1,0:T(8,128)(2,1)S(1)}, f32[256,4352]{1,0:T(8,128)}) fusion(f32[256,4352]{1,0:T(8,128)} %convolution_add_fusion.1, bf16[256,1088]{0,1:T(8,128)(2,1)S(1)} %get-tuple-element.146, bf16[4352,1088]{1,0:T(8,128)(2,1)} %all-gather.12.cloned.1.call-done), kind=kOutput, calls=%fused_computation.69 | convolution fusion | flops 2506747648 | bytes 21185536 | tf_op jit(solution)/shard_map/dot_general | solution.py:20
  288.8 9.0 %multiply_reduce_fusion.1 = (f32[1088]{0:T(1024)S(1)}, f32[256]{0:T(256)S(1)}, f32[256]{0:T(256)S(1)}, f32[1088]{0:T(1024)S(1)}, f32[256,1088]{0,1:T(8,128)S(1)}) fusion(f32[256,1088]{0,1:T(8,128)S(1)} %get-tuple-element.175, f32[256]{0:T(256)S(1)} %add_rsqrt_fusion, f32[256]{0:T(256)S(1)} %broadcast_multiply_fusion.4, f32[1088]{0:T(1024)S(1)} %get-tuple-element.165, ...), kind=kOutput, calls=%fused_computation.117 | convolution fusion | flops 2426811904 | bytes 13943552 | tf_op jit(solution)/shard_map/dot_general | solution.py:20
  302.3 107.8 %while.27 = (s32[]{:T(128)}, bf16[17,256,64]{1,2,0:T(8,128)(2,1)}, bf16[17,256,64]{1,2,0:T(8,128)(2,1)}, bf16[17,256,64]{1,2,0:T(8,128)(2,1)}, s32[256]{0:T(256)...) while((s32[]{:T(128)}, bf16[17,256,64]{1,2,0:T(8,128)(2,1)}, ...), condition=%wide.region_14.15_spmd, body=%wide.region_12.14_spmd.sunk | while | flops 42794752 | bytes 2633841 | solution.py:171
  438.4 88.6 %all-to-all-done = bf16[256,4,3264]{0,2,1:T(8,128)(2,1)} async-done(((bf16[256,4,3264]{0,2,1:T(8,128)(2,1)}), bf16[256,4,3264]{0,2,1:T(8,128)(2,1)}, u32[]{:S(2)}, u32[]{:S(2)}) %all-to-all-start) | async-done | bytes 6684704 | tf_op jit(solution)/shard_map/all_to_all | solution.py:198
  527.0 27.7 %copy.42 = bf16[4,256,3264]{1,0,2:T(4,128)(2,1)} copy(bf16[4,256,3264]{1,2,0:T(8,128)(2,1)} %bitcast.41) | data formatting | bytes 13369344 | tf_op jit(solution)/shard_map/all_to_all | solution.py:198
  554.7 12.7 %reshape.184 = bf16[1024,8,408]{0,2,1:T(8,128)(2,1)} reshape(bf16[4,256,3264]{1,0,2:T(4,128)(2,1)} %copy.42) | data formatting | bytes 13369344 | tf_op jit(solution)/shard_map/reshape | solution.py:199
  567.4 6.2 fusion.87
  573.6 7.6 fusion.93
  584.0 7.8 fusion.92
  591.8 7.3 convolution_add_fusion
  600.7 6.5 fusion.94
  609.2 8.1 fusion.78
  617.4 40.4 %all-reduce.2 = f32[13056]{0:T(1024)S(1)} all-reduce(f32[13056]{0:T(1024)S(1)} %concatenate.21), channel_id=3, replica_groups=mesh['fsdp'=8,'rep'=4] {'fsdp','rep'}, use_global_device_ids=true, to_apply=%region_26.27.clone | all-reduce | flops 13056 | bytes 104448
  661.4 8.7 fusion.62
  670.1 11.5 %reduce-scatter.12.cloned.1.call-done = f32[136,1088]{1,0:T(8,128)} async-done(((f32[1088,1088]{1,0:T(8,128)}), f32[136,1088]{1,0:T(8,128)}) %reduce-scatter.12.cloned.1.call-update) | async-done | bytes 591888
  681.6 103.8 %reduce-scatter.10.cloned.1.call-done = f32[136,1088]{1,0:T(8,128)} async-done(((f32[1088,1088]{1,0:T(8,128)}), f32[136,1088]{1,0:T(8,128)}) %reduce-scatter.10.cloned.1.call-update) | async-done | bytes 591888
  785.3 103.0 %reduce-scatter.14.cloned.1.call-done = f32[136,1088]{1,0:T(8,128)} async-done(((f32[1088,1088]{1,0:T(8,128)}), f32[136,1088]{1,0:T(8,128)}) %reduce-scatter.14.cloned.1.call-update) | async-done | bytes 591888
  (318 shorter events, 204.8 us)
Async XLA Ops:
  7.2 48.8 %copy-start.2 = (bf16[256,1088]{0,1:T(8,128)(2,1)S(1)}, bf16[256,1088]{0,1:T(8,128)(2,1)}, u32[]{:S(2)}) copy-start(bf16[256,1088]{0,1:T(8,128)(2,1)} %param.11) | copy-start | bytes 1671172
  7.2 48.6 %copy-start.18 = (s32[1,4]{1,0:T(1,128)S(1)}, s32[1,4]{1,0:T(1,128)}, u32[]{:S(2)}) copy-start(s32[1,4]{1,0:T(1,128)} %param.12) | copy-start | bytes 52
  7.2 92.0 %all-gather.8.cloned.1.call-start = ((), (), s32[]{:S(2)}) async-start(), calls=%async_computation.4 | async-start | bytes 10340352 | tf_op jit(solution)/shard_map/all_gather | solution.py:96
  7.9 177.3 %all-gather.10.cloned.1.call-start = ((), (), s32[]{:S(2)}) async-start(), calls=%async_computation.5 | async-start | bytes 10340352 | tf_op jit(solution)/shard_map/all_gather | solution.py:138
  8.7 262.8 %all-gather.12.cloned.1.call-start = ((), (), s32[]{:S(2)}) async-start(), calls=%async_computation.6 | async-start | bytes 10340352 | tf_op jit(solution)/shard_map/all_gather | solution.py:139
  9.4 564.2 %all-gather.18.cloned.1.call-start = ((), (), s32[]{:S(2)}) async-start(), calls=%async_computation.9 | async-start | bytes 2785280 | tf_op jit(solution)/shard_map/all_gather | solution.py:220
  56.4 48.3 %copy-start.13 = (bf16[256,1088]{0,1:T(8,128)(2,1)}, bf16[256,1088]{0,1:T(8,128)(2,1)S(1)}, u32[]{:S(2)}) copy-start(bf16[256,1088]{0,1:T(8,128)(2,1)S(1)} %fusion.72) | copy-start | bytes 1671172
  146.4 3.2 copy-start.15
  146.4 3.2 copy-start.17
  149.6 3.6 copy-start.4
  151.0 34.2 %copy-start.11 = (bf16[256,1088]{0,1:T(8,128)(2,1)S(1)}, bf16[256,1088]{0,1:T(8,128)(2,1)}, u32[]{:S(2)}) copy-start(bf16[256,1088]{0,1:T(8,128)(2,1)} %add_convert_fusion.1) | copy-start | bytes 1671172
  151.0 433.0 %all-gather.14.cloned.1.call-start = ((), (), s32[]{:S(2)}) async-start(), calls=%async_computation.7 | async-start | bytes 2785280 | tf_op jit(solution)/shard_map/all_gather | solution.py:218
  151.6 440.2 %all-gather.16.cloned.1.call-start = ((), (), s32[]{:S(2)}) async-start(), calls=%async_computation.8 | async-start | bytes 2785280 | tf_op jit(solution)/shard_map/all_gather | solution.py:219
  153.5 118.0 %copy-start.14 = (bf16[256,1088]{0,1:T(8,128)(2,1)}, bf16[256,1088]{0,1:T(8,128)(2,1)S(1)}, u32[]{:S(2)}) copy-start(bf16[256,1088]{0,1:T(8,128)(2,1)S(1)} %get-tuple-element.146) | copy-start | bytes 1671172
  288.8 9.0 %copy-start.12 = (bf16[256,4352]{1,0:T(8,128)(2,1)}, bf16[256,4352]{1,0:T(8,128)(2,1)S(1)}, u32[]{:S(2)}) copy-start(bf16[256,4352]{1,0:T(8,128)(2,1)S(1)} %get-tuple-element.148) | copy-start | bytes 6684676
  297.8 3.7 copy-start.6
  432.3 94.7 %all-to-all-start = ((bf16[256,4,3264]{0,2,1:T(8,128)(2,1)}), bf16[256,4,3264]{0,2,1:T(8,128)(2,1)}, u32[]{:S(2)}, u32[]{:S(2)}) async-start(bf16[256,4,3264]{0,2,1:T(8,128)(2,1)} %bitcast.151), calls=%async_computation | async-start | bytes 13369344 | tf_op jit(solution)/shard_map/all_to_all | solution.py:198
  437.6 161.5 %all-gather.20.cloned.1.call-start = ((), (), s32[]{:S(2)}) async-start(), calls=%async_computation.10 | async-start | bytes 2785280 | tf_op jit(solution)/shard_map/all_gather | solution.py:221
  438.4 243.2 %reduce-scatter.12.cloned.1.call-start = ((), (), s32[]{:S(2)}) async-start(), calls=%async_computation.12 | async-start | bytes 5640192
  581.2 204.1 %reduce-scatter.10.cloned.1.call-start = ((), (), s32[]{:S(2)}) async-start(), calls=%async_computation.11 | async-start | bytes 5640192
  584.0 7.8 copy-start.9
  599.1 289.3 %reduce-scatter.14.cloned.1.call-start = ((), (), s32[]{:S(2)}) async-start(), calls=%async_computation.13 | async-start | bytes 5640192
  609.2 49.2 %copy-start.5 = (bf16[256,1088]{0,1:T(8,128)(2,1)S(1)}, bf16[256,1088]{0,1:T(8,128)(2,1)}, u32[]{:S(2)}) copy-start(bf16[256,1088]{0,1:T(8,128)(2,1)} %param.17) | copy-start | bytes 1671172
  609.2 49.2 %copy-start.7 = (f32[256,1088]{0,1:T(8,128)S(1)}, f32[256,1088]{0,1:T(8,128)}, u32[]{:S(2)}) copy-start(f32[256,1088]{0,1:T(8,128)} %copy-done.6) | copy-start | bytes 3342340
  (6 other events, 14.9 us)
Sparse Core Ops, SparseCore 0:
  10.9 88.1 all-gather.7
  102.1 83.1 all-gather.9
  188.2 83.2 all-gather.11
  273.4 22.1 all-gather.17
  297.6 23.5 all-gather.13
  422.9 24.7 all-gather.15
  449.3 37.3 all-gather.19
  581.3 100.1 reduce-scatter.11
  686.2 99.0 reduce-scatter.9
  789.4 98.9 reduce-scatter.13

commit v2 on v1

v2 whole, which is shorter than its diff:
```python
import jax
import jax.numpy as jnp
from jax import lax
from jax.experimental import pallas as pl
from jax.experimental.pallas import tpu as pltpu
from jax.sharding import PartitionSpec as P

HEADS = 17
HEAD_DIM = 64
FF = 4352
LANES = 128

epsilon = 1e-05
negative = -1e30
factor = HEAD_DIM ** (-0.5)
both = ("fsdp", "rep")


def contract(left, right, left_dim, right_dim):
    return lax.dot_general(
        left, right, (((left_dim,), (right_dim,)), ((), ())), preferred_element_type=jnp.float32
    )


def normalize(values):
    center = values - jnp.mean(values, axis=1, keepdims=True)
    scaled = lax.rsqrt(jnp.mean(center * center, axis=1, keepdims=True) + epsilon)
    return (center * scaled, scaled)


def norm_back(grad_normed, normed, scaled, gain):
    scaled_grad = grad_normed * gain
    return scaled * (
        scaled_grad
        - jnp.mean(scaled_grad, axis=1, keepdims=True)
        - normed * jnp.mean(scaled_grad * normed, axis=1, keepdims=True)
    )


def visible(key_segment, query_segment):
    shape = (key_segment.shape[0], query_segment.shape[1])
    key_ids = lax.broadcasted_iota(jnp.int32, shape, 0)
    query_ids = lax.broadcasted_iota(jnp.int32, shape, 1)
    return (key_segment == query_segment) & (key_ids <= query_ids)


def head_rows(part, head):
    return pl.ds((part * HEADS + head) * HEAD_DIM, HEAD_DIM)


def forward_kernel(qkv_ref, key_seg_ref, query_seg_ref, mixed_ref, total_ref):
    allowed = visible(key_seg_ref[...], query_seg_ref[...])
    for head in range(HEADS):
        queries = qkv_ref[head_rows(0, head), :]
        keys = qkv_ref[head_rows(1, head), :]
        values = qkv_ref[head_rows(2, head), :]
        scores = jnp.where(allowed, contract(keys.T, queries, 1, 0) * factor, negative)
        peak = jnp.max(scores, axis=0, keepdims=True)
        exp_scores = jnp.exp(scores - peak)
        total = jnp.sum(exp_scores, axis=0, keepdims=True)
        probs = (exp_scores / total).astype(jnp.bfloat16)
        mixed_ref[head_rows(0, head), :] = contract(values, probs, 1, 0).astype(jnp.bfloat16)
        total_ref[pl.ds(head, 1), :] = peak + jnp.log(total)


def backward_kernel(qkv_ref, total_ref, grad_ref, key_seg_ref, query_seg_ref, out_ref):
    allowed = visible(key_seg_ref[...], query_seg_ref[...])
    for head in range(HEADS):
        queries = qkv_ref[head_rows(0, head), :]
        keys = qkv_ref[head_rows(1, head), :]
        values = qkv_ref[head_rows(2, head), :]
        grads = grad_ref[head_rows(0, head), :]
        scores = contract(keys.T, queries, 1, 0) * factor
        probs = jnp.where(allowed, jnp.exp(scores - total_ref[pl.ds(head, 1), :]), 0.0)
        grad_probs = contract(values.T, grads, 1, 0)
        delta = jnp.sum(probs * grad_probs, axis=0, keepdims=True)
        grad_scores = (probs * (grad_probs - delta) * factor).astype(jnp.bfloat16)
        out_ref[head_rows(0, head), :] = contract(keys, grad_scores, 1, 0).astype(jnp.bfloat16)
        out_ref[head_rows(1, head), :] = contract(queries, grad_scores, 1, 1).astype(jnp.bfloat16)
        out_ref[head_rows(2, head), :] = contract(
            grads, probs.astype(jnp.bfloat16), 1, 1
        ).astype(jnp.bfloat16)


def on_chip(body, outs, args, flops):
    return pl.pallas_call(
        body,
        out_shape=outs,
        compiler_params=pltpu.CompilerParams(vmem_limit_bytes=32 * 2**20),
        cost_estimate=pl.CostEstimate(flops=flops, bytes_accessed=6 * 2**20, transcendentals=2**20),
    )(*args)


def local(tokens, lengths, attn_weights, vectors, up_weights, down_weights, cotangent):
    outer_count = lax.axis_size("fsdp")
    inner_count = lax.axis_size("rep")
    device_count = outer_count * inner_count
    slot_count, model_width = tokens.shape
    shard_rows = attn_weights.shape[0]
    vector_size = vectors.shape[0]
    vector_rows = -(-vector_size // (16 * model_width)) * 16
    vector_rows = vector_rows - (shard_rows % 16) if shard_rows % 16 else vector_rows
    packed_vectors = jnp.pad(vectors, (0, vector_rows * model_width - vector_size))
    packed = jnp.concatenate([attn_weights, packed_vectors.reshape(vector_rows, model_width)], axis=0)
    packed_full = lax.all_gather(packed, both, axis=0)
    up_full = lax.all_gather(up_weights, both, axis=0, tiled=True)
    down_full = lax.all_gather(down_weights, both, axis=0, tiled=True)
    attn_full = packed_full[:, :shard_rows].reshape(device_count * shard_rows, model_width)
    vector_full = packed_full[:, shard_rows:].reshape(device_count, vector_rows * model_width)
    params = vector_full[:, :vector_size].reshape(device_count * vector_size).astype(jnp.float32)
    qkv_full = attn_full[: 3 * model_width]
    out_full = attn_full[3 * model_width :]
    gain_one = params[0:model_width]
    shift_one = params[model_width : 2 * model_width]
    query_bias = params[2 * model_width : 3 * model_width]
    value_bias = params[3 * model_width : 4 * model_width]
    out_bias = params[4 * model_width : 5 * model_width]
    gain_two = params[5 * model_width : 6 * model_width]
    shift_two = params[6 * model_width : 7 * model_width]
    up_bias = params[7 * model_width : 7 * model_width + FF]
    down_bias = params[7 * model_width + FF :]

    seq_count = lengths.shape[1]
    upto = lax.iota(jnp.int32, seq_count)[:, None] >= lax.iota(jnp.int32, seq_count)[None, :]
    seq_ends = jnp.sum(jnp.where(upto, lengths, 0), axis=1)
    positions = lax.iota(jnp.int32, slot_count)
    segment = jnp.sum((positions[:, None] >= seq_ends[None, :]).astype(jnp.int32), axis=1)
    live_rows = (positions < seq_ends[-1]).astype(jnp.float32)[:, None]
    key_segment, query_segment = segment[:, None], segment[None, :]

    inputs = tokens.astype(jnp.float32)
    normed_one, scaled_one = normalize(inputs)
    hidden_one = (normed_one * gain_one + shift_one).astype(jnp.bfloat16)
    qkv_bias = jnp.concatenate([query_bias, jnp.zeros_like(query_bias), value_bias])
    qkv = (contract(qkv_full, hidden_one, 1, 1) + qkv_bias[:, None]).astype(jnp.bfloat16)
    mixed, totals = on_chip(
        forward_kernel,
        (
            jax.ShapeDtypeStruct((model_width, slot_count), jnp.bfloat16),
            jax.ShapeDtypeStruct((HEADS, slot_count), jnp.float32),
        ),
        (qkv, key_segment, query_segment),
        4 * slot_count * slot_count * model_width,
    )
    residual = inputs + contract(mixed, out_full, 0, 1) + out_bias
    normed_two, scaled_two = normalize(residual)
    hidden_two = (normed_two * gain_two + shift_two).astype(jnp.bfloat16)
    grad_output = cotangent.astype(jnp.float32) * live_rows
    grad_down_in = grad_output.astype(jnp.bfloat16)

    def to_all(right):
        copies = jnp.broadcast_to(right[None], (inner_count,) + right.shape)
        return lax.all_to_all(copies, "rep", split_axis=0, concat_axis=0, tiled=True)

    right_down = to_all(grad_down_in)
    right_one = to_all(hidden_one)
    right_mixed = to_all(mixed.T)
    up_full, right_down, right_one = lax.optimization_barrier((up_full, right_down, right_one))
    upward = contract(up_full, hidden_two, 1, 1) + up_bias[:, None]

    def gelu_exact(values):
        return jax.nn.gelu(values, approximate=False)

    activated, gelu_vjp = jax.vjp(gelu_exact, upward)
    activated = activated.astype(jnp.bfloat16)
    def to_owners(left):
        blocks = left.reshape(outer_count, inner_count, shard_rows, slot_count)
        blocks = blocks.transpose(1, 0, 2, 3).reshape(
            inner_count * outer_count * shard_rows, slot_count
        )
        return lax.all_to_all(blocks, "rep", split_axis=0, concat_axis=0, tiled=True).reshape(
            inner_count, outer_count * shard_rows, slot_count
        )

    def owner_grad(left, right):
        return sum(contract(left[i], right[i], 1, 0) for i in range(inner_count))

    def summed(partial):
        return lax.psum_scatter(
            partial.astype(jnp.bfloat16), "fsdp", scatter_dimension=0, tiled=True
        )

    act_rows = to_owners(activated)
    down_full, act_rows, right_mixed = lax.optimization_barrier((down_full, act_rows, right_mixed))
    right_two = to_all(hidden_two)
    down_shard = summed(owner_grad(act_rows, right_down))

    output = (residual + contract(activated, down_full, 0, 0) + down_bias) * live_rows
    grad_down_bias = jnp.sum(grad_down_in.astype(jnp.float32), axis=0)
    grad_act = contract(down_full, grad_down_in, 1, 1)
    grad_upward = gelu_vjp(grad_act)[0]
    grad_up_in = grad_upward.astype(jnp.bfloat16)
    grad_up_bias = jnp.sum(grad_up_in.astype(jnp.float32), axis=1)

    up_shard = summed(owner_grad(to_owners(grad_up_in), right_two))

    grad_hidden_two = contract(grad_up_in, up_full, 0, 0)
    grad_gain_two = jnp.sum(grad_hidden_two * normed_two, axis=0)
    grad_shift_two = jnp.sum(grad_hidden_two, axis=0)
    grad_residual = grad_output + norm_back(grad_hidden_two, normed_two, scaled_two, gain_two)
    grad_attended = grad_residual.astype(jnp.bfloat16)
    grad_out_bias = jnp.sum(grad_attended.astype(jnp.float32), axis=0)
    grad_mixed = contract(out_full, grad_attended, 0, 1).astype(jnp.bfloat16)
    grad_qkv = on_chip(
        backward_kernel,
        jax.ShapeDtypeStruct((3 * model_width, slot_count), jnp.bfloat16),
        (qkv, totals, grad_mixed, key_segment, query_segment),
        10 * slot_count * slot_count * model_width,
    )

    attn_left = to_owners(jnp.concatenate([grad_qkv, grad_attended.T], axis=0))
    feature_ids = (
        (lax.iota(jnp.int32, outer_count)[:, None] * inner_count + lax.axis_index("rep"))
        * shard_rows
        + lax.iota(jnp.int32, shard_rows)[None, :]
    ).reshape(1, outer_count * shard_rows, 1)
    is_projection = feature_ids < 3 * model_width
    zero_low = jnp.zeros_like(attn_left)
    attn_total = owner_grad(jnp.where(is_projection, attn_left, zero_low), right_one) + owner_grad(
        jnp.where(is_projection, zero_low, attn_left), right_mixed
    )
    attn_shard = summed(attn_total)

    bias_sums = jnp.sum(grad_qkv.astype(jnp.float32), axis=1)
    grad_hidden_one = contract(grad_qkv, qkv_full, 0, 0)
    grad_gain_one = jnp.sum(grad_hidden_one * normed_one, axis=0)
    grad_shift_one = jnp.sum(grad_hidden_one, axis=0)
    grad_inputs = grad_residual + norm_back(grad_hidden_one, normed_one, scaled_one, gain_one)

    grad_params = jnp.concatenate(
        [
            grad_gain_one,
            grad_shift_one,
            bias_sums[:model_width],
            bias_sums[2 * model_width :],
            grad_out_bias,
            grad_gain_two,
            grad_shift_two,
            grad_up_bias,
            grad_down_bias,
        ]
    )
    per_device = -(-vector_size // LANES) * LANES
    padded = jnp.pad(
        grad_params.reshape(device_count, vector_size), ((0, 0), (0, per_device - vector_size))
    )
    terms = lax.all_to_all(padded, both, split_axis=0, concat_axis=0, tiled=True)
    vector_shard = jnp.sum(terms, axis=0)[:vector_size]
    return (
        output.astype(jnp.bfloat16),
        grad_inputs.astype(jnp.bfloat16),
        attn_shard.astype(jnp.float32),
        vector_shard,
        up_shard.astype(jnp.float32),
        down_shard.astype(jnp.float32),
    )


def solution(mesh):
    rows = P(both, None)
    return jax.shard_map(
        local,
        mesh=mesh,
        in_specs=(rows, rows, rows, P(both), rows, rows, rows),
        out_specs=(rows, rows, rows, P(both), rows, rows),
        check_vma=False,
    )
```

time: 907 us -> 605 us (0.67)
  matrix products: 237 us -> 94 us
  waiting for transfers between devices: 460 us -> 360 us
  blocking collectives: 83.2 us -> 30.7 us
  local copies, waits for them, and re-layouts: 66.5 us -> 33.4 us
  starting transfers between devices: 5.92 us -> 31.3 us
  Pallas kernels: 0 us -> 11.3 us
    dot_general x131 -> x24, matrix products: 237 us -> 94 us  [contract(): lax.dot_general(left, right, (((left_dim,), (right_dim,)), ((), ())), pre...]
    unnamed x13 -> x9, waiting for transfers between devices: 222 us -> 108 us
    unnamed x2 -> x0, blocking collectives: 83.2 us -> none
    all_gather x7 -> x3, waiting for transfers between devices: 150 us -> 210 us  [the longest x1 87 us: local(): packed_full = lax.all_gather(packed, both, axis=0)]
    all_to_all x1 -> x7, waiting for transfers between devices: 88.6 us -> 40.9 us  [the longest x4 24.3 us: to_all(): lax.all_to_all(copies, 'rep', split_axis=0, concat_axis=0, tiled=True)]
    all_to_all x0 -> x1, blocking collectives: none -> 30.7 us  [to_owners(): lax.all_to_all(blocks, 'rep', split_axis=0, concat_axis=0, tiled=True)]
    all_to_all x1, local copies, waits for them, and re-layouts: 27.7 us -> 0.68 us  [local(): lax.all_to_all(padded, both, split_axis=0, concat_axis=0, tiled=True)]
    all_to_all x1 -> x7, starting transfers between devices: 5.31 us -> 30.8 us  [the longest x4 18.3 us: to_all(): lax.all_to_all(copies, 'rep', split_axis=0, concat_axis=0, tiled=True)]
  transfers between devices with their start and end apart: 11 -> 13, of which waited for: 7 -> 8; matrix products, arithmetic and copies ran while one was open for 37% -> 18% of each run, Pallas kernels for 0% -> 1%
where the time goes in v2:
time: 605 us; the launch traced here: 595 us
  waiting for transfers between devices  360 us (60%)
  matrix products  94 us (16%)
  local copies, waits for them, and re-layouts  33.4 us (6%)
  starting transfers between devices  31.3 us (5%)
  blocking collectives  30.7 us (5%)
  other arithmetic  19.8 us (3%)
  between operations  15.1 us (2%)
  Pallas kernels  11.3 us (2%)
    unnamed x9, waiting for transfers between devices  108 us
    dot_general x24, matrix products, contract(): lax.dot_general(left, right, (((left_dim,), (right_dim,)), ((), ())), pre...  94 us
    all_gather x1, waiting for transfers between devices, local(): packed_full = lax.all_gather(packed, both, axis=0)  87 us
    all_gather x1, waiting for transfers between devices, local(): down_full = lax.all_gather(down_weights, both, axis=0, tiled=True)  74.2 us
    all_gather x1, waiting for transfers between devices, local(): up_full = lax.all_gather(up_weights, both, axis=0, tiled=True)  49.2 us
    all_to_all x1, blocking collectives, to_owners(): lax.all_to_all(blocks, 'rep', split_axis=0, concat_axis=0, tiled=True)  30.7 us
    all_to_all x4, waiting for transfers between devices, to_all(): lax.all_to_all(copies, 'rep', split_axis=0, concat_axis=0, tiled=True)  24.3 us
    all_to_all x4, starting transfers between devices, to_all(): lax.all_to_all(copies, 'rep', split_axis=0, concat_axis=0, tiled=True)  18.3 us
  transfers between devices with their start and end apart: 13, of which 8 were waited for; matrix products, arithmetic and copies ran while one was open for 18% of the time, Pallas kernels for 1%

profile of v2, /device:TPU:0, one launch (start us, length us, event | category | flops | bytes accessed | tf_op | source)
XLA Modules:
  0.0 595.2 jit_solution(2344320922608353664)
XLA Ops:
  17.4 4.3 all-to-all-start
  22.9 87.0 %all-gather.9.cloned.1.call-done = bf16[4608,1088]{1,0:T(8,128)(2,1)} async-done(((bf16[144,1088]{1,0:T(8,128)(2,1)}), bf16[4608,1088]{1,0:T(8,128)(2,1)}) %all-gather.9.cloned.1.call-update) | async-done | bytes 10027024 | tf_op jit(solution)/shard_map/all_gather | solution.py:105
  111.1 6.8 %slice.228 = bf16[24,136,1088]{2,1,0:T(8,128)(2,1)} slice(bf16[32,144,1088]{2,1,0:T(8,128)(2,1)} %bitcast.140), slice={[0:24], [0:136], [0:1088]} | slice | bytes 14204928 | tf_op jit(solution)/shard_map/slice | solution.py:111
  124.7 4.5 all-to-all-start.1
  129.2 5.6 fusion.4.qkv_ref
  137.6 5.2 shard_map.118
  145.1 20.2 %all-to-all-done.1 = bf16[4,256,1088]{1,2,0:T(8,128)(2,1)} async-done(((bf16[4,256,1088]{1,2,0:T(8,128)(2,1)}), bf16[4,256,1088]{1,2,0:T(8,128)(2,1)}, u32[]{:S(2)}, u32[]{:S(2)}) %all-to-all-start.1) | async-done | bytes 2228256 | tf_op jit(solution)/shard_map/all_to_all | solution.py:153
  166.8 5.0 all-to-all-start.3
  171.8 49.2 %all-gather.5.cloned.1.call-done = bf16[4352,1088]{1,0:T(8,128)(2,1)} async-done(((bf16[136,1088]{1,0:T(8,128)(2,1)}), bf16[4352,1088]{1,0:T(8,128)(2,1)}) %all-gather.5.cloned.1.call-update) | async-done | bytes 9469968 | tf_op jit(solution)/shard_map/all_gather | solution.py:106
  221.0 15.9 %multiply_convert_fusion = (bf16[4352,256]{1,0:T(8,128)(2,1)S(1)}, f32[4352,256]{1,0:T(8,128)}, f32[4352,256]{1,0:T(8,128)}) fusion(f32[4352]{0:T(1024)S(1)} %copy-done.19, bf16[4352,1088]{1,0:T(8,128)(2,1)} %all-gather.5.cloned.1.call-done, bf16[256,1088]{0,1:T(8,128)(2,1)S(1)} %copy-done.10), kind=kOutput, calls=%fused_computation.23 | convolution fusion | flops 2497839104 | bytes 21185536 | tf_op jit(solution)/shard_map/dot_general | solution.py:20
  239.8 4.6 all-to-all-start.2
  244.8 74.2 %all-gather.7.cloned.1.call-done = bf16[4352,1088]{1,0:T(8,128)(2,1)} async-done(((bf16[136,1088]{1,0:T(8,128)(2,1)}), bf16[4352,1088]{1,0:T(8,128)(2,1)}) %all-gather.7.cloned.1.call-update) | async-done | bytes 9469968 | tf_op jit(solution)/shard_map/all_gather | solution.py:107
  319.0 11.4 %convert_reduce_fusion = (f32[4352]{0:T(1024)}, bf16[4352,256]{1,0:T(8,128)(2,1)S(1)}) fusion(f32[4352,256]{1,0:T(8,128)} %get-tuple-element.37, f32[4352,256]{1,0:T(8,128)} %get-tuple-element.54, bf16[4352,1088]{1,0:T(8,128)(2,1)} %all-gather.7.cloned.1.call-done, bf16[256,1088]{0,1:T(8,128)(2,1)S(1)} %copy-done.15), kind=kOutput, calls=%fused_computation.21 | convolution fusion | flops 2442129152 | bytes 21185536 | tf_op jit(solution)/shard_map/dot_general | solution.py:20
  330.4 9.7 %multiply_reduce_fusion = (f32[1088]{0:T(1024)}, f32[256]{0:T(256)S(1)}, f32[256]{0:T(256)S(1)}, f32[1088]{0:T(1024)}, f32[256,1088]{0,1:T(8,128)S(1)}) fusion(f32[256,1088]{0,1:T(8,128)S(1)} %get-tuple-element.53, f32[256]{0:T(256)S(1)} %add_rsqrt_fusion, f32[256]{0:T(256)S(1)} %broadcast_multiply_fusion.4, f32[1088]{0:T(1024)S(1)} %get-tuple-element.44, ...), kind=kOutput, calls=%fused_computation.66 | convolution fusion | flops 2426811904 | bytes 13943552 | tf_op jit(solution)/shard_map/dot_general | solution.py:20
  342.8 6.1 %shard_map.119 = bf16[3264,256]{1,0:T(8,128)(2,1)S(1)} custom-call(bf16[3264,256]{1,0:T(8,128)(2,1)S(1)} %fusion.4.qkv_ref, f32[17,256]{1,0:T(8,128)S(1)} %get-tuple-element.17.total_ref, bf16[1088,256]{1,0:T(8,128)(2,1)S(1)} %convolution_convert_fusion.grad_ref, s32[256,1]{1,0:T(8,128)S(1)} %copy.31.key_seg_ref, s32[1,256]{1,0:T(1,128)S(1)} %bitcast.138), custom_call_target="tpu_custom_call" | custom-call | flops 713031680 | bytes 6291456 | tf_op jit(solution)/shard_map/pallas_call | solution.py:86
  355.4 4.5 all-to-all-start.4
  366.3 3.5 fusion.3
  370.5 16.6 %all-to-all-done.4 = bf16[4,1088,256]{2,1,0:T(8,128)(2,1)} async-done(((bf16[4,1088,256]{2,1,0:T(8,128)(2,1)}), bf16[4,1088,256]{2,1,0:T(8,128)(2,1)}, u32[]{:S(2)}, u32[]{:S(2)}) %all-to-all-start.4) | async-done | bytes 2228256 | tf_op jit(solution)/shard_map/all_to_all | solution.py:171
  388.6 4.5 all-to-all-start.7
  416.2 4.1 all-to-all-done.7
  420.3 30.7 %all_to_all.56 = bf16[4,1088,256]{2,1,0:T(8,128)(2,1)S(1)} all-to-all(bf16[4,1088,256]{2,1,0:T(8,128)(2,1)} %bitcast.144), channel_id=1, replica_groups=mesh['fsdp'=8,'rep'=4] {'rep'}, dimensions={0} | all-to-all | bytes 4456448 | tf_op jit(solution)/shard_map/all_to_all | solution.py:171
  465.5 9.4 %fusion.14 = bf16[256,1088]{0,1:T(8,128)(2,1)} fusion(f32[256,1088]{0,1:T(8,128)S(1)} %copy-done.1, bf16[4352,256]{1,0:T(8,128)(2,1)} %copy-done.12, bf16[4352,1088]{1,0:T(8,128)(2,1)} %all-gather.7.cloned.1.call-done, f32[1088]{0:T(1024)S(1)} %copy-done.24, f32[256]{0:T(256)S(1)} %copy-done.30), kind=kOutput, calls=%fused_computation.43 | convolution fusion | flops 2425421824 | bytes 13374720 | tf_op jit(solution)/shard_map/dot_general | solution.py:20
  477.4 36.5 %reduce-scatter.10.cloned.1.call-done = bf16[136,1088]{1,0:T(8,128)(2,1)} async-done(((bf16[1088,1088]{1,0:T(8,128)(2,1)}), bf16[136,1088]{1,0:T(8,128)(2,1)}) %reduce-scatter.10.cloned.1.call-update) | async-done | bytes 295952
  515.8 70.3 %reduce-scatter.12.cloned.1.call-done = bf16[136,1088]{1,0:T(8,128)(2,1)} async-done(((bf16[1088,1088]{1,0:T(8,128)(2,1)}), bf16[136,1088]{1,0:T(8,128)(2,1)}) %reduce-scatter.12.cloned.1.call-update) | async-done | bytes 295952
  (159 shorter events, 90.3 us)
Async XLA Ops:
  7.2 102.8 %all-gather.9.cloned.1.call-start = ((), (), s32[]{:S(2)}) async-start(), calls=%async_computation.13 | async-start | bytes 10948608 | tf_op jit(solution)/shard_map/all_gather | solution.py:105
  9.7 211.2 %all-gather.5.cloned.1.call-start = ((), (), s32[]{:S(2)}) async-start(), calls=%async_computation.11 | async-start | bytes 10340352 | tf_op jit(solution)/shard_map/all_gather | solution.py:106
  10.5 308.5 %all-gather.7.cloned.1.call-start = ((), (), s32[]{:S(2)}) async-start(), calls=%async_computation.12 | async-start | bytes 10340352 | tf_op jit(solution)/shard_map/all_gather | solution.py:107
  17.4 105.0 %all-to-all-start = ((bf16[4,256,1088]{1,2,0:T(8,128)(2,1)}), bf16[4,256,1088]{1,2,0:T(8,128)(2,1)S(1)}, u32[]{:S(2)}, u32[]{:S(2)}) async-start(bf16[4,256,1088]{1,2,0:T(8,128)(2,1)} %broadcast_in_dim.44), calls=%async_computation | async-start | bytes 4456448 | tf_op jit(solution)/shard_map/all_to_all | solution.py:153
  22.1 87.8 %copy-start.21 = (f32[256]{0:T(256)}, f32[256]{0:T(256)S(1)}, u32[]{:S(2)}) copy-start(f32[256]{0:T(256)S(1)} %broadcast_multiply_fusion.5) | copy-start | bytes 3076
  124.7 40.6 %all-to-all-start.1 = ((bf16[4,256,1088]{1,2,0:T(8,128)(2,1)}), bf16[4,256,1088]{1,2,0:T(8,128)(2,1)}, u32[]{:S(2)}, u32[]{:S(2)}) async-start(bf16[4,256,1088]{1,2,0:T(8,128)(2,1)} %broadcast_in_dim.45), calls=%async_computation.1 | async-start | bytes 4456448 | tf_op jit(solution)/shard_map/all_to_all | solution.py:153
  134.8 8.0 %copy-start.27 = (f32[1088]{0:T(1024)S(1)}, f32[1088]{0:T(1024)}, u32[]{:S(2)}) copy-start(f32[1088]{0:T(1024)} %get-tuple-element.45) | copy-start | bytes 13060
  143.7 196.4 %copy-start = (f32[256,1088]{0,1:T(8,128)}, f32[256,1088]{0,1:T(8,128)S(1)}, u32[]{:S(2)}) copy-start(f32[256,1088]{0,1:T(8,128)S(1)} %get-tuple-element.53) | copy-start | bytes 3342340
  166.8 54.2 %copy-start.10 = (bf16[256,1088]{0,1:T(8,128)(2,1)S(1)}, bf16[256,1088]{0,1:T(8,128)(2,1)}, u32[]{:S(2)}) copy-start(bf16[256,1088]{0,1:T(8,128)(2,1)} %add_convert_fusion.1) | copy-start | bytes 1671172
  166.8 54.2 %copy-start.19 = (f32[4352]{0:T(1024)S(1)}, f32[4352]{0:T(1024)}, u32[]{:S(2)}) copy-start(f32[4352]{0:T(1024)} %slice.238) | copy-start | bytes 52228
  166.8 73.0 %all-to-all-start.3 = ((bf16[4,256,1088]{1,2,0:T(8,128)(2,1)}), bf16[4,256,1088]{1,2,0:T(8,128)(2,1)}, u32[]{:S(2)}, u32[]{:S(2)}) async-start(bf16[4,256,1088]{1,2,0:T(8,128)(2,1)} %broadcast_in_dim.46), calls=%async_computation.3 | async-start | bytes 4456448 | tf_op jit(solution)/shard_map/all_to_all | solution.py:153
  239.8 79.3 %copy-start.15 = (bf16[256,1088]{0,1:T(8,128)(2,1)S(1)}, bf16[256,1088]{0,1:T(8,128)(2,1)}, u32[]{:S(2)}) copy-start(bf16[256,1088]{0,1:T(8,128)(2,1)} %copy-done.14) | copy-start | bytes 1671172
  239.8 79.3 %all-to-all-start.2 = ((bf16[4,1088,256]{2,1,0:T(8,128)(2,1)}), bf16[4,1088,256]{2,1,0:T(8,128)(2,1)}, u32[]{:S(2)}, u32[]{:S(2)}) async-start(bf16[4,1088,256]{2,1,0:T(8,128)(2,1)} %bitcast.143), calls=%async_computation.2 | async-start | bytes 4456448 | tf_op jit(solution)/shard_map/all_to_all | solution.py:171
  330.4 9.7 %copy-start.13 = (bf16[4352,256]{1,0:T(8,128)(2,1)}, bf16[4352,256]{1,0:T(8,128)(2,1)S(1)}, u32[]{:S(2)}) copy-start(bf16[4352,256]{1,0:T(8,128)(2,1)S(1)} %get-tuple-element.33) | copy-start | bytes 6684676
  330.4 9.7 %copy-start.9 = (bf16[256,1088]{0,1:T(8,128)(2,1)S(1)}, bf16[256,1088]{0,1:T(8,128)(2,1)}, u32[]{:S(2)}) copy-start(bf16[256,1088]{0,1:T(8,128)(2,1)} %param.13) | copy-start | bytes 1671172
  330.4 9.7 %copy-start.29 = (f32[256]{0:T(256)S(1)}, f32[256]{0:T(256)}, u32[]{:S(2)}) copy-start(f32[256]{0:T(256)} %copy-done.28) | copy-start | bytes 3076
  340.1 8.8 %slice-start = ((s8[7520256]{0:T(1024)(128)(4,1)}), s8[4194304]{0:T(1024)(128)(4,1)S(1)}, s32[]{:S(2)}) async-start(s8[7520256]{0:T(1024)(128)(4,1)} %bitcast.147), calls=%async_computation.17 | async-start | bytes 8388608
  355.4 31.6 %all-to-all-start.4 = ((bf16[4,1088,256]{2,1,0:T(8,128)(2,1)}), bf16[4,1088,256]{2,1,0:T(8,128)(2,1)}, u32[]{:S(2)}, u32[]{:S(2)}) async-start(bf16[4,1088,256]{2,1,0:T(8,128)(2,1)} %bitcast.142), calls=%async_computation.4 | async-start | bytes 4456448 | tf_op jit(solution)/shard_map/all_to_all | solution.py:171
  359.9 115.7 %reduce-scatter.14.cloned.1.call-start = ((), (), s32[]{:S(2)}) async-start(), calls=%async_computation.16 | async-start | bytes 2820096
  369.8 17.3 %copy-start.11 = (bf16[256,1088]{0,1:T(8,128)(2,1)S(1)}, bf16[256,1088]{0,1:T(8,128)(2,1)}, u32[]{:S(2)}) copy-start(bf16[256,1088]{0,1:T(8,128)(2,1)} %add_convert_fusion.1) | copy-start | bytes 1671172
  388.6 31.7 %all-to-all-start.7 = ((bf16[4,256,1088]{1,2,0:T(8,128)(2,1)}), bf16[4,256,1088]{1,2,0:T(8,128)(2,1)}, u32[]{:S(2)}, u32[]{:S(2)}) async-start(bf16[4,256,1088]{1,2,0:T(8,128)(2,1)} %broadcast_in_dim.49), calls=%async_computation.7 | async-start | bytes 4456448 | tf_op jit(solution)/shard_map/all_to_all | solution.py:153
  393.1 120.8 %reduce-scatter.10.cloned.1.call-start = ((), (), s32[]{:S(2)}) async-start(), calls=%async_computation.14 | async-start | bytes 2820096
  413.0 173.1 %reduce-scatter.12.cloned.1.call-start = ((), (), s32[]{:S(2)}) async-start(), calls=%async_computation.15 | async-start | bytes 2820096
  462.0 12.9 %all-to-all-start.5 = ((f32[32,1,512]{2,1,0:T(1,128)}), f32[32,1,512]{2,1,0:T(1,128)S(1)}, u32[]{:S(2)}, u32[]{:S(2)}) async-start(f32[32,1,512]{2,1,0:T(1,128)} %all_to_all.43), calls=%async_computation.5 | async-start | bytes 131072 | tf_op jit(solution)/shard_map/all_to_all | solution.py:247
  (23 other events, 80.1 us)
Sparse Core Ops, SparseCore 0:
  11.5 98.4 all-gather.8
  112.9 108.0 all-gather.4
  223.9 95.1 all-gather.6
  369.9 70.2 reduce-scatter.13
  443.6 70.2 reduce-scatter.9
  517.4 68.6 reduce-scatter.11
